TPU v7x, 32 devices: a whole 2x2x4 slice. The times are simulated.
32 devices in a mesh: lon: 8 (over z, x), lat: 4 (over y, core).
Axes of the slice: x: 2, y: 2, z: 4, core: 2. Of those that a mesh axis runs over, the one named last changes fastest.
Arguments:
- state: float32 [4, 4, 128, 2048], P(None, None, 'lat', 'lon'), may hold values from -3 to 3
- cotangent: float32 [4, 4, 128, 2048], P(None, None, 'lat', 'lon'), may hold values from -6 to 6
- seamask: int32 [128, 2048], P('lat', 'lon'), may hold values 0 or 1
- levels: int32 [128, 2048], P('lat', 'lon'), may hold values from 1 to 4
Outputs:
- final_state: float32 [4, 4, 128, 2048], P(None, None, 'lat', 'lon')
- adjoint_state: float32 [4, 4, 128, 2048], P(None, None, 'lat', 'lon')
All inputs are finite; a program needn't handle non-finite values. No bound on the sum of `seamask` on one device may be relied on, other than what follows from the above.
Results may differ from a plain program's by a relative error of at most 0.0003.
Values sent between devices are 32-bit elements; how exact they have to be, the bound alone decides.
A program may use at most 64 MiB of HBM per device.

v0:
```python
import jax
import jax.numpy as jnp
from jax import lax
from jax.sharding import PartitionSpec as P

courant = 0.4
vert_mix = 0.1
rotation = 0.3
buoyancy = 0.3
bottom_drag = 0.2


def padded_2(block, sides, width):
    for axis, dim in sides:
        count = lax.axis_size(axis)
        forward = [(i, i + 1) for i in range(count - 1)]
        forward.append((count - 1, 0))
        backward = [(target, source) for source, target in forward]
        low = lax.ppermute(
            lax.slice_in_dim(block, block.shape[dim] - width, None, axis=dim), axis, forward
        )
        high = lax.ppermute(lax.slice_in_dim(block, 0, width, axis=dim), axis, backward)
        block = jnp.concatenate([low, block, high], axis=dim)
    return block


def slab_of(values, start, length, along):
    return lax.slice_in_dim(values, start, start + length, axis=values.ndim + along)


def face_div(fields, speeds, wet_mask, along):
    extent = fields.shape[along]
    faces = extent - 5
    cells = [slab_of(fields, offset, faces, along) for offset in range(6)]
    face_speed = 0.5 * (slab_of(speeds, 2, faces, along) + slab_of(speeds, 3, faces, along))
    open_face = slab_of(wet_mask, 2, faces, along) * slab_of(wet_mask, 3, faces, along)
    central = (
        37.0 * (cells[2] + cells[3]) - 8.0 * (cells[1] + cells[4]) + (cells[0] + cells[5])
    ) / 60.0
    damping = (
        10.0 * (cells[3] - cells[2]) - 5.0 * (cells[4] - cells[1]) + (cells[5] - cells[0])
    ) / 60.0
    flux = open_face * (face_speed * central - jnp.sqrt(face_speed * face_speed + 0.0001) * damping)
    return slab_of(flux, 1, faces - 1, along) - slab_of(flux, 0, faces - 1, along)


def advance(padded, sea_rim, level_rim, first_row, lat_total):
    level_count = padded.shape[1]
    lat_cells = padded.shape[2]
    lon_cells = padded.shape[3]
    level_index = jnp.arange(level_count, dtype=jnp.int32)[:, None, None]
    wet_mask = (sea_rim[None] * (level_index < level_rim[None]).astype(jnp.int32)).astype(
        jnp.float32
    )
    bottom = (sea_rim[None] * (level_index == level_rim[None] - 1).astype(jnp.int32)).astype(
        jnp.float32
    )
    divergence = face_div(padded, padded[2], wet_mask, -1)[:, :, 3 : lat_cells - 3, :]
    divergence = divergence + face_div(padded, padded[3], wet_mask, -2)[:, :, :, 3 : lon_cells - 3]
    center = padded[:, :, 3 : lat_cells - 3, 3 : lon_cells - 3]
    wet_center = wet_mask[:, 3 : lat_cells - 3, 3 : lon_cells - 3]
    bottom_center = bottom[:, 3 : lat_cells - 3, 3 : lon_cells - 3]
    zero_level = jnp.zeros_like(center[:, :1])
    zero_wet = jnp.zeros_like(wet_center[:1])
    above_cells = jnp.concatenate([zero_level, center[:, :-1]], axis=1)
    below_cells = jnp.concatenate([center[:, 1:], zero_level], axis=1)
    wet_above = jnp.concatenate([zero_wet, wet_center[:-1]], axis=0)
    wet_below = jnp.concatenate([wet_center[1:], zero_wet], axis=0)
    vertical = vert_mix * (wet_above * (above_cells - center) + wet_below * (below_cells - center))
    density = (-0.2 * padded[0] + 0.8 * padded[1]) * wet_mask
    pressure = buoyancy * jnp.cumsum(density, axis=0)
    press_east = 0.5 * (
        pressure[:, 3 : lat_cells - 3, 4 : lon_cells - 2]
        - pressure[:, 3 : lat_cells - 3, 2 : lon_cells - 4]
    )
    press_north = 0.5 * (
        pressure[:, 4 : lat_cells - 2, 3 : lon_cells - 3]
        - pressure[:, 2 : lat_cells - 4, 3 : lon_cells - 3]
    )
    row_index = (first_row + 3 + jnp.arange(lat_cells - 6, dtype=jnp.int32)).astype(jnp.float32)
    latitude = jnp.pi * ((row_index + 0.5) / lat_total - 0.5)
    coriolis = (rotation * jnp.sin(latitude))[:, None]
    east_now = center[2]
    north_now = center[3]
    force_east = coriolis * north_now - press_east - bottom_drag * bottom_center * east_now
    force_north = -coriolis * east_now - press_north - bottom_drag * bottom_center * north_now
    forcing = jnp.concatenate(
        [jnp.zeros_like(center[:2]), jnp.stack([force_east, force_north])], axis=0
    )
    return (center - courant * divergence + vertical + forcing) * wet_center[None]


def extend(values, rim_depth):
    return padded_2(values, (("lon", 3), ("lat", 2)), rim_depth)


def inside_rows(lat_start, rim_depth, row_count, lat_total):
    global_row = lat_start - rim_depth + jnp.arange(row_count + 2 * rim_depth, dtype=jnp.int32)
    return ((global_row >= 0) & (global_row < lat_total))[:, None]


def fold_back(gradient, rim_depth):
    lat_cells = gradient.shape[2]
    row_count = lat_cells - 2 * rim_depth
    edges = jnp.concatenate(
        [gradient[:, :, :rim_depth], gradient[:, :, lat_cells - rim_depth :]], axis=2
    )
    arrived = padded_2(edges, (("lat", 2),), rim_depth)
    core = gradient[:, :, rim_depth : lat_cells - rim_depth]
    core = core.at[:, :, :rim_depth].add(arrived[:, :, :rim_depth])
    core = core.at[:, :, row_count - rim_depth :].add(arrived[:, :, 3 * rim_depth :])
    lon_cells = core.shape[3]
    col_count = lon_cells - 2 * rim_depth
    sides = jnp.concatenate([core[..., :rim_depth], core[..., lon_cells - rim_depth :]], axis=3)
    received = padded_2(sides, (("lon", 3),), rim_depth)
    result = core[..., rim_depth : lon_cells - rim_depth]
    result = result.at[..., :rim_depth].add(received[..., :rim_depth])
    result = result.at[..., col_count - rim_depth :].add(received[..., 3 * rim_depth :])
    return result


def shards(state, cotangent, seamask, levels):
    row_count = state.shape[2]
    lat_total = row_count * lax.axis_size("lat")
    lat_start = lax.axis_index("lat") * row_count
    rim_depth = 3
    int_rims = padded_2(jnp.stack([seamask, levels]), (("lon", 2), ("lat", 1)), rim_depth)
    inside = inside_rows(lat_start, rim_depth, row_count, lat_total)
    inside_float = inside.astype(jnp.float32)
    sea_rim = int_rims[0] * inside.astype(jnp.int32)
    level_rim = int_rims[1]

    def one_step(padded):
        return advance(padded, sea_rim, level_rim, lat_start - 3, lat_total)

    state_one, back_first = jax.vjp(one_step, extend(state, 3) * inside_float)
    final_state, back_second = jax.vjp(one_step, extend(state_one, 3) * inside_float)
    middle = fold_back(back_second(cotangent)[0] * inside_float, 3)
    adjoint_state = fold_back(back_first(middle)[0] * inside_float, 3)
    return (final_state, adjoint_state)


def solution(mesh):
    placed = (
        P(None, None, "lat", "lon"),
        P(None, None, "lat", "lon"),
        P("lat", "lon"),
        P("lat", "lon"),
    )
    return jax.shard_map(
        shards,
        mesh=mesh,
        in_specs=placed,
        out_specs=(P(None, None, "lat", "lon"), P(None, None, "lat", "lon")),
        check_vma=False,
    )
```

profile of v0, /device:TPU:1, one launch (start us, length us, event | category | flops | bytes accessed | tf_op | source)
XLA Modules:
  0.0 147.7 jit_solution(2951464710622694472)
XLA Ops:
  1.5 2.0 %collective-permute-start.4 = (s32[2,32,3]{2,1,0:T(8,128)S(1)}, s32[2,32,3]{2,1,0:T(8,128)S(1)}, u32[]{:S(2)}, u32[]{:S(2)}) collective-permute-start(s32[2,32,3]{2,1,0:T(8,128)S(1)} %get-tuple-element.254), channel_id=1, source_target_pairs={{0,4},{4,8},{8,12},{12,16},{16,20},{20,24},{24,28},{28,0},{1,5},{5... | collective-permute-start | bytes 2312 | tf_op jit(solution)/shard_map/ppermute | solution.py:19
  3.5 3.1 %collective-permute-start.5 = (s32[2,32,3]{2,1,0:T(8,128)S(1)}, s32[2,32,3]{2,1,0:T(8,128)S(1)}, u32[]{:S(2)}, u32[]{:S(2)}) collective-permute-start(s32[2,32,3]{2,1,0:T(8,128)S(1)} %get-tuple-element.255), channel_id=1, source_target_pairs={{4,0},{8,4},{12,8},{16,12},{20,16},{24,20},{28,24},{0,28},{5,1},{9... | collective-permute-start | bytes 2312 | tf_op jit(solution)/shard_map/ppermute | solution.py:22
  7.9 4.1 %collective-permute-start.1 = (f32[4,4,32,3]{3,2,1,0:T(8,128)S(1)}, f32[4,4,32,3]{3,2,1,0:T(8,128)S(1)}, u32[]{:S(2)}, u32[]{:S(2)}) collective-permute-start(f32[4,4,32,3]{3,2,1,0:T(8,128)S(1)} %get-tuple-element.227), channel_id=1, source_target_pairs={{4,0},{8,4},{12,8},{16,12},{20,16},{24,20},{28,24},{0,28},{5,1},{9... | collective-permute-start | bytes 18440 | tf_op jit(solution)/shard_map/ppermute | solution.py:22
  12.3 2.8 %collective-permute-start.6 = (s32[2,3,262]{2,1,0:T(4,128)S(1)}, s32[2,3,262]{2,1,0:T(4,128)S(1)}, u32[]{:S(2)}, u32[]{:S(2)}) collective-permute-start(s32[2,3,262]{2,1,0:T(4,128)S(1)} %get-tuple-element.245), channel_id=1, source_target_pairs={{0,1},{1,2},{2,3},{3,0},{4,5},{5,6},{6,7},{7,4},{8,9},{9,10},{10,1... | collective-permute-start | bytes 18872 | tf_op jit(solution)/shard_map/ppermute | solution.py:19
  15.1 3.4 %collective-permute-done = f32[4,4,32,3]{3,2,1,0:T(8,128)S(1)} collective-permute-done((f32[4,4,32,3]{3,2,1,0:T(8,128)S(1)}, f32[4,4,32,3]{3,2,1,0:T(8,128)S(1)}, u32[]{:S(2)}, u32[]{:S(2)}) %collective-permute-start) | collective-permute-done | bytes 6176 | tf_op jit(solution)/shard_map/ppermute | solution.py:19
  18.4 1.9 %collective-permute-done.1 = f32[4,4,32,3]{3,2,1,0:T(8,128)S(1)} collective-permute-done((f32[4,4,32,3]{3,2,1,0:T(8,128)S(1)}, f32[4,4,32,3]{3,2,1,0:T(8,128)S(1)}, u32[]{:S(2)}, u32[]{:S(2)}) %collective-permute-start.1) | collective-permute-done | bytes 6176 | tf_op jit(solution)/shard_map/ppermute | solution.py:22
  20.6 3.0 %collective-permute-start.2 = (f32[4,4,3,262]{3,2,1,0:T(4,128)S(1)}, f32[4,4,3,262]{3,2,1,0:T(4,128)S(1)}, u32[]{:S(2)}, u32[]{:S(2)}) collective-permute-start(f32[4,4,3,262]{3,2,1,0:T(4,128)S(1)} %get-tuple-element.162), channel_id=1, source_target_pairs={{0,1},{1,2},{2,3},{3,0},{4,5},{5,6},{6,7},{7,4},{8,9},{9,10},{10,1... | collective-permute-start | bytes 150920 | tf_op jit(solution)/shard_map/ppermute | solution.py:19
  25.5 2.2 %collective-permute-done.3 = f32[4,4,3,262]{3,2,1,0:T(4,128)S(1)} collective-permute-done((f32[4,4,3,262]{3,2,1,0:T(4,128)S(1)}, f32[4,4,3,262]{3,2,1,0:T(4,128)S(1)}, u32[]{:S(2)}, u32[]{:S(2)}) %collective-permute-start.3) | collective-permute-done | bytes 50336 | tf_op jit(solution)/shard_map/ppermute | solution.py:22
  29.6 2.6 %subtract_multiply_fusion.3 = (f32[4,4,38,257]{3,2,1,0:T(8,128)S(1)}, f32[4,4,38,257]{3,2,1,0:T(8,128)}, f32[4,4,38,257]{3,2,1,0:T(8,128)}) fusion(f32[4,38,257]{2,1,0:T(8,128)S(1)} %fusion.49, f32[4,38,257]{2,1,0:T(8,128)S(1)} %get-tuple-element.242, f32[4,38,257]{2,1,0:T(8,128)S(1)} %slice_multiply_fusion.7, f32[4,4,38,262]{3,2,1,0:T(8,128)S(1)} %maximum_multiply_fusion), kind=kLoop, calls=%fused_computation.43 | loop fusion | flops 2812608 | bytes 6093984 | tf_op jit(solution)/shard_map/jvp()/mul | solution.py:43
  33.4 2.2 %subtract_multiply_fusion.2 = (f32[4,4,33,262]{3,2,1,0:T(8,128)S(1)}, f32[4,4,33,262]{3,2,1,0:T(8,128)}, f32[4,4,33,262]{3,2,1,0:T(8,128)}) fusion(f32[4,33,262]{2,1,0:T(8,128)S(1)} %fusion.48, f32[4,33,262]{2,1,0:T(8,128)S(1)} %get-tuple-element.243, f32[4,33,262]{2,1,0:T(8,128)S(1)} %slice_multiply_fusion.6, f32[4,4,38,262]{3,2,1,0:T(8,128)S(1)} %maximum_multiply_fusion), kind=kLoop, calls=%fused_computation.40 | loop fusion | flops 2490048 | bytes 5395104 | tf_op jit(solution)/shard_map/jvp()/mul | solution.py:43
  38.7 4.1 %collective-permute-start.9 = (f32[4,4,32,3]{3,2,1,0:T(8,128)S(1)}, f32[4,4,32,3]{3,2,1,0:T(8,128)S(1)}, u32[]{:S(2)}, u32[]{:S(2)}) collective-permute-start(f32[4,4,32,3]{3,2,1,0:T(8,128)S(1)} %get-tuple-element.225), channel_id=1, source_target_pairs={{4,0},{8,4},{12,8},{16,12},{20,16},{24,20},{28,24},{0,28},{5,1},{9... | collective-permute-start | bytes 18440 | tf_op jit(solution)/shard_map/ppermute | solution.py:22
  44.3 5.5 %collective-permute-done.8 = f32[4,4,32,3]{3,2,1,0:T(8,128)S(1)} collective-permute-done((f32[4,4,32,3]{3,2,1,0:T(8,128)S(1)}, f32[4,4,32,3]{3,2,1,0:T(8,128)S(1)}, u32[]{:S(2)}, u32[]{:S(2)}) %collective-permute-start.8) | collective-permute-done | bytes 6176 | tf_op jit(solution)/shard_map/ppermute | solution.py:19
  49.8 2.2 %collective-permute-done.9 = f32[4,4,32,3]{3,2,1,0:T(8,128)S(1)} collective-permute-done((f32[4,4,32,3]{3,2,1,0:T(8,128)S(1)}, f32[4,4,32,3]{3,2,1,0:T(8,128)S(1)}, u32[]{:S(2)}, u32[]{:S(2)}) %collective-permute-start.9) | collective-permute-done | bytes 6176 | tf_op jit(solution)/shard_map/ppermute | solution.py:22
  55.5 2.2 %collective-permute-done.11 = f32[4,4,3,262]{3,2,1,0:T(4,128)S(1)} collective-permute-done((f32[4,4,3,262]{3,2,1,0:T(4,128)S(1)}, f32[4,4,3,262]{3,2,1,0:T(4,128)S(1)}, u32[]{:S(2)}, u32[]{:S(2)}) %collective-permute-start.11) | collective-permute-done | bytes 50336 | tf_op jit(solution)/shard_map/ppermute | solution.py:22
  60.5 2.9 %multiply_add_fusion.10 = (f32[4,4,33,262]{3,2,1,0:T(8,128)S(1)}, f32[4,4,33,262]{3,2,1,0:T(8,128)S(1)}, f32[4,4,33,262]{3,2,1,0:T(8,128)S(1)}, f32[4,4,33,262]{...) fusion(f32[4,4,33,262]{3,2,1,0:T(8,128)S(1)} %get-tuple-element, ...), kind=kLoop, calls=%fused_computation.62 | loop fusion | flops 5187600 | bytes 8300160 | tf_op jit(solution)/shard_map/transpose(jvp())/add_any | solution.py:38
  65.5 2.5 %multiply_add_fusion.7 = (f32[4,4,38,257]{3,2,1,0:T(8,128)S(1)}, f32[4,4,38,257]{3,2,1,0:T(8,128)S(1)}, f32[4,4,38,257]{3,2,1,0:T(8,128)S(1)}, f32[4,4,38,257]{3...) fusion(f32[4,4,38,257]{3,2,1,0:T(8,128)S(1)} %get-tuple-element, ...), kind=kLoop, calls=%fused_computation.57 | loop fusion | flops 5859600 | bytes 9375360 | tf_op jit(solution)/shard_map/transpose(jvp())/add_any | solution.py:38
  83.2 3.6 %collective-permute-start.15 = (f32[4,4,32,3]{3,2,1,0:T(8,128)}, f32[4,4,32,3]{3,2,1,0:T(8,128)}, u32[]{:S(2)}, u32[]{:S(2)}) collective-permute-start(f32[4,4,32,3]{3,2,1,0:T(8,128)} %get-tuple-element.198), channel_id=1, source_target_pairs={{4,0},{8,4},{12,8},{16,12},{20,16},{24,20},{28,24},{0,28},{5,1},{9... | collective-permute-start | bytes 18440 | tf_op jit(solution)/shard_map/ppermute | solution.py:22
  86.8 5.5 %collective-permute-done.14 = f32[4,4,32,3]{3,2,1,0:T(8,128)S(1)} collective-permute-done((f32[4,4,32,3]{3,2,1,0:T(8,128)S(1)}, f32[4,4,32,3]{3,2,1,0:T(8,128)S(1)}, u32[]{:S(2)}, u32[]{:S(2)}) %collective-permute-start.14) | collective-permute-done | bytes 6176 | tf_op jit(solution)/shard_map/ppermute | solution.py:19
  95.1 2.2 %collective-permute-done.15 = f32[4,4,32,3]{3,2,1,0:T(8,128)} collective-permute-done((f32[4,4,32,3]{3,2,1,0:T(8,128)}, f32[4,4,32,3]{3,2,1,0:T(8,128)}, u32[]{:S(2)}, u32[]{:S(2)}) %collective-permute-start.15) | collective-permute-done | bytes 6176 | tf_op jit(solution)/shard_map/ppermute | solution.py:22
  99.2 3.6 %scatter-add.31 = f32[4,4,32,256]{3,2,1,0:T(8,128)S(1)} dynamic-update-slice(f32[4,4,32,256]{3,2,1,0:T(8,128)S(1)} %copy-done.12, f32[4,4,32,3]{3,2,1,0:T(8,128)} %slice_add_fusion.2, s32[]{:T(128)} %constant.268.clone.1, s32[]{:T(128)} %constant.268.clone.1, s32[]{:T(128)} %constant.268.clone.1, s32[]{:T(128)} %constant.292.clone.1) | dynamic-update-slice | bytes 12292 | tf_op jit(solution)/shard_map/scatter-add | solution.py:118
  128.2 2.8 %fusion.11 = f32[4,4,32,256]{3,2,1,0:T(8,128)} fusion(f32[4,4,32,262]{3,2,1,0:T(8,128)} %get-tuple-element.187, f32[4,4,32,262]{3,2,1,0:T(8,128)S(1)} %get-tuple-element.186, f32[4,4,38,256]{3,2,1,0:T(8,128)} %get-tuple-element.183, f32[4,4,38,256]{3,2,1,0:T(8,128)S(1)} %copy-done.20, f32[1,4,32,256]{3,2,1,0:T(8,128)} %get-tuple-element.157, ...), kind=kLoop, calls=%fused_computation.80 | loop fusion | flops 2097152 | bytes 4587536 | tf_op jit(solution)/shard_map/jvp()/mul | solution.py:90
  131.2 4.1 %collective-permute-start.19 = (f32[4,4,32,3]{3,2,1,0:T(8,128)}, f32[4,4,32,3]{3,2,1,0:T(8,128)S(1)}, u32[]{:S(2)}, u32[]{:S(2)}) collective-permute-start(f32[4,4,32,3]{3,2,1,0:T(8,128)} %get-tuple-element.196), channel_id=1, source_target_pairs={{4,0},{8,4},{12,8},{16,12},{20,16},{24,20},{28,24},{0,28},{5,1},{9... | collective-permute-start | bytes 18440 | tf_op jit(solution)/shard_map/ppermute | solution.py:22
  137.2 6.8 %collective-permute-done.19 = f32[4,4,32,3]{3,2,1,0:T(8,128)S(1)} collective-permute-done((f32[4,4,32,3]{3,2,1,0:T(8,128)}, f32[4,4,32,3]{3,2,1,0:T(8,128)S(1)}, u32[]{:S(2)}, u32[]{:S(2)}) %collective-permute-start.19) | collective-permute-done | bytes 6176 | tf_op jit(solution)/shard_map/ppermute | solution.py:22
  144.2 2.7 %scatter-add.39 = f32[4,4,32,256]{3,2,1,0:T(8,128)S(1)} dynamic-update-slice(f32[4,4,32,256]{3,2,1,0:T(8,128)S(1)} %scatter-add.36, f32[4,4,32,3]{3,2,1,0:T(8,128)S(1)} %slice_add_fusion, s32[]{:T(128)} %constant.268.clone.1, s32[]{:T(128)} %constant.268.clone.1, s32[]{:T(128)} %constant.268.clone.1, s32[]{:T(128)} %constant.292.clone.1) | dynamic-update-slice | bytes 12292 | tf_op jit(solution)/shard_map/scatter-add | solution.py:118
  (228 shorter events, 67.9 us)
Async XLA Ops:
  1.5 10.7 %collective-permute-start.4 = (s32[2,32,3]{2,1,0:T(8,128)S(1)}, s32[2,32,3]{2,1,0:T(8,128)S(1)}, u32[]{:S(2)}, u32[]{:S(2)}) collective-permute-start(s32[2,32,3]{2,1,0:T(8,128)S(1)} %get-tuple-element.254), channel_id=1, source_target_pairs={{0,4},{4,8},{8,12},{12,16},{16,20},{20,24},{24,28},{28,0},{1,5},{5... | collective-permute-start | bytes 2312 | tf_op jit(solution)/shard_map/ppermute | solution.py:19
  3.5 8.6 %collective-permute-start.5 = (s32[2,32,3]{2,1,0:T(8,128)S(1)}, s32[2,32,3]{2,1,0:T(8,128)S(1)}, u32[]{:S(2)}, u32[]{:S(2)}) collective-permute-start(s32[2,32,3]{2,1,0:T(8,128)S(1)} %get-tuple-element.255), channel_id=1, source_target_pairs={{4,0},{8,4},{12,8},{16,12},{20,16},{24,20},{28,24},{0,28},{5,1},{9... | collective-permute-start | bytes 2312 | tf_op jit(solution)/shard_map/ppermute | solution.py:22
  7.8 10.7 %collective-permute-start = (f32[4,4,32,3]{3,2,1,0:T(8,128)S(1)}, f32[4,4,32,3]{3,2,1,0:T(8,128)S(1)}, u32[]{:S(2)}, u32[]{:S(2)}) collective-permute-start(f32[4,4,32,3]{3,2,1,0:T(8,128)S(1)} %get-tuple-element.226), channel_id=1, source_target_pairs={{0,4},{4,8},{8,12},{12,16},{16,20},{20,24},{24,28},{28,0},{1,5},{5... | collective-permute-start | bytes 18440 | tf_op jit(solution)/shard_map/ppermute | solution.py:19
  7.9 12.5 %collective-permute-start.1 = (f32[4,4,32,3]{3,2,1,0:T(8,128)S(1)}, f32[4,4,32,3]{3,2,1,0:T(8,128)S(1)}, u32[]{:S(2)}, u32[]{:S(2)}) collective-permute-start(f32[4,4,32,3]{3,2,1,0:T(8,128)S(1)} %get-tuple-element.227), channel_id=1, source_target_pairs={{4,0},{8,4},{12,8},{16,12},{20,16},{24,20},{28,24},{0,28},{5,1},{9... | collective-permute-start | bytes 18440 | tf_op jit(solution)/shard_map/ppermute | solution.py:22
  12.1 25.4 %copy-start.46 = (f32[32]{0:T(128)}, f32[32]{0:T(128)S(1)}, u32[]{:S(2)}) copy-start(f32[32]{0:T(128)S(1)} %get-tuple-element.257) | copy-start | bytes 388
  12.1 57.0 %copy-start.49 = (f32[38]{0:T(128)}, f32[38]{0:T(128)S(1)}, u32[]{:S(2)}) copy-start(f32[38]{0:T(128)S(1)} %fusion.89) | copy-start | bytes 460
  12.3 11.4 %collective-permute-start.6 = (s32[2,3,262]{2,1,0:T(4,128)S(1)}, s32[2,3,262]{2,1,0:T(4,128)S(1)}, u32[]{:S(2)}, u32[]{:S(2)}) collective-permute-start(s32[2,3,262]{2,1,0:T(4,128)S(1)} %get-tuple-element.245), channel_id=1, source_target_pairs={{0,1},{1,2},{2,3},{3,0},{4,5},{5,6},{6,7},{7,4},{8,9},{9,10},{10,1... | collective-permute-start | bytes 18872 | tf_op jit(solution)/shard_map/ppermute | solution.py:19
  15.1 8.6 %collective-permute-start.7 = (s32[2,3,262]{2,1,0:T(4,128)S(1)}, s32[2,3,262]{2,1,0:T(4,128)S(1)}, u32[]{:S(2)}, u32[]{:S(2)}) collective-permute-start(s32[2,3,262]{2,1,0:T(4,128)S(1)} %get-tuple-element.246), channel_id=1, source_target_pairs={{1,0},{2,1},{3,2},{0,3},{5,4},{6,5},{7,6},{4,7},{9,8},{10,9},{11,1... | collective-permute-start | bytes 18872 | tf_op jit(solution)/shard_map/ppermute | solution.py:22
  20.6 4.9 %collective-permute-start.2 = (f32[4,4,3,262]{3,2,1,0:T(4,128)S(1)}, f32[4,4,3,262]{3,2,1,0:T(4,128)S(1)}, u32[]{:S(2)}, u32[]{:S(2)}) collective-permute-start(f32[4,4,3,262]{3,2,1,0:T(4,128)S(1)} %get-tuple-element.162), channel_id=1, source_target_pairs={{0,1},{1,2},{2,3},{3,0},{4,5},{5,6},{6,7},{7,4},{8,9},{9,10},{10,1... | collective-permute-start | bytes 150920 | tf_op jit(solution)/shard_map/ppermute | solution.py:19
  23.6 4.0 %collective-permute-start.3 = (f32[4,4,3,262]{3,2,1,0:T(4,128)S(1)}, f32[4,4,3,262]{3,2,1,0:T(4,128)S(1)}, u32[]{:S(2)}, u32[]{:S(2)}) collective-permute-start(f32[4,4,3,262]{3,2,1,0:T(4,128)S(1)} %get-tuple-element.163), channel_id=1, source_target_pairs={{1,0},{2,1},{3,2},{0,3},{5,4},{6,5},{7,6},{4,7},{9,8},{10,9},{11,1... | collective-permute-start | bytes 150920 | tf_op jit(solution)/shard_map/ppermute | solution.py:22
  23.8 48.0 %copy-start.17 = (s32[38,262]{1,0:T(8,128)}, s32[38,262]{1,0:T(8,128)S(1)}, u32[]{:S(2)}) copy-start(s32[38,262]{1,0:T(8,128)S(1)} %get-tuple-element.249) | copy-start | bytes 119476
  24.2 35.9 %copy-start.8 = (f32[4,33,262]{2,1,0:T(8,128)}, f32[4,33,262]{2,1,0:T(8,128)S(1)}, u32[]{:S(2)}) copy-start(f32[4,33,262]{2,1,0:T(8,128)S(1)} %slice_multiply_fusion.6) | copy-start | bytes 415012
  38.6 11.2 %collective-permute-start.8 = (f32[4,4,32,3]{3,2,1,0:T(8,128)S(1)}, f32[4,4,32,3]{3,2,1,0:T(8,128)S(1)}, u32[]{:S(2)}, u32[]{:S(2)}) collective-permute-start(f32[4,4,32,3]{3,2,1,0:T(8,128)S(1)} %get-tuple-element.224), channel_id=1, source_target_pairs={{0,4},{4,8},{8,12},{12,16},{16,20},{20,24},{24,28},{28,0},{1,5},{5... | collective-permute-start | bytes 18440 | tf_op jit(solution)/shard_map/ppermute | solution.py:19
  38.7 13.3 %collective-permute-start.9 = (f32[4,4,32,3]{3,2,1,0:T(8,128)S(1)}, f32[4,4,32,3]{3,2,1,0:T(8,128)S(1)}, u32[]{:S(2)}, u32[]{:S(2)}) collective-permute-start(f32[4,4,32,3]{3,2,1,0:T(8,128)S(1)} %get-tuple-element.225), channel_id=1, source_target_pairs={{4,0},{8,4},{12,8},{16,12},{20,16},{24,20},{28,24},{0,28},{5,1},{9... | collective-permute-start | bytes 18440 | tf_op jit(solution)/shard_map/ppermute | solution.py:22
  52.2 3.3 %collective-permute-start.10 = (f32[4,4,3,262]{3,2,1,0:T(4,128)S(1)}, f32[4,4,3,262]{3,2,1,0:T(4,128)S(1)}, u32[]{:S(2)}, u32[]{:S(2)}) collective-permute-start(f32[4,4,3,262]{3,2,1,0:T(4,128)S(1)} %get-tuple-element.160), channel_id=1, source_target_pairs={{0,1},{1,2},{2,3},{3,0},{4,5},{5,6},{6,7},{7,4},{8,9},{9,10},{10,1... | collective-permute-start | bytes 150920 | tf_op jit(solution)/shard_map/ppermute | solution.py:19
  53.7 4.0 %collective-permute-start.11 = (f32[4,4,3,262]{3,2,1,0:T(4,128)S(1)}, f32[4,4,3,262]{3,2,1,0:T(4,128)S(1)}, u32[]{:S(2)}, u32[]{:S(2)}) collective-permute-start(f32[4,4,3,262]{3,2,1,0:T(4,128)S(1)} %get-tuple-element.161), channel_id=1, source_target_pairs={{1,0},{2,1},{3,2},{0,3},{5,4},{6,5},{7,6},{4,7},{9,8},{10,9},{11,1... | collective-permute-start | bytes 150920 | tf_op jit(solution)/shard_map/ppermute | solution.py:22
  71.6 1.9 %collective-permute-start.12 = (f32[4,4,3,262]{3,2,1,0:T(4,128)S(1)}, f32[4,4,3,262]{3,2,1,0:T(4,128)S(1)}, u32[]{:S(2)}, u32[]{:S(2)}) collective-permute-start(f32[4,4,3,262]{3,2,1,0:T(4,128)S(1)} %get-tuple-element.171), channel_id=1, source_target_pairs={{0,1},{1,2},{2,3},{3,0},{4,5},{5,6},{6,7},{7,4},{8,9},{9,10},{10,1... | collective-permute-start | bytes 150920 | tf_op jit(solution)/shard_map/ppermute | solution.py:19
  72.7 4.4 %collective-permute-start.13 = (f32[4,4,3,262]{3,2,1,0:T(4,128)}, f32[4,4,3,262]{3,2,1,0:T(4,128)}, u32[]{:S(2)}, u32[]{:S(2)}) collective-permute-start(f32[4,4,3,262]{3,2,1,0:T(4,128)} %get-tuple-element.170), channel_id=1, source_target_pairs={{1,0},{2,1},{3,2},{0,3},{5,4},{6,5},{7,6},{4,7},{9,8},{10,9},{11,1... | collective-permute-start | bytes 150920 | tf_op jit(solution)/shard_map/ppermute | solution.py:22
  80.6 11.6 %collective-permute-start.14 = (f32[4,4,32,3]{3,2,1,0:T(8,128)S(1)}, f32[4,4,32,3]{3,2,1,0:T(8,128)S(1)}, u32[]{:S(2)}, u32[]{:S(2)}) collective-permute-start(f32[4,4,32,3]{3,2,1,0:T(8,128)S(1)} %get-tuple-element.199), channel_id=1, source_target_pairs={{0,4},{4,8},{8,12},{12,16},{16,20},{20,24},{24,28},{28,0},{1,5},{5... | collective-permute-start | bytes 18440 | tf_op jit(solution)/shard_map/ppermute | solution.py:19
  83.2 14.1 %collective-permute-start.15 = (f32[4,4,32,3]{3,2,1,0:T(8,128)}, f32[4,4,32,3]{3,2,1,0:T(8,128)}, u32[]{:S(2)}, u32[]{:S(2)}) collective-permute-start(f32[4,4,32,3]{3,2,1,0:T(8,128)} %get-tuple-element.198), channel_id=1, source_target_pairs={{4,0},{8,4},{12,8},{16,12},{20,16},{24,20},{28,24},{0,28},{5,1},{9... | collective-permute-start | bytes 18440 | tf_op jit(solution)/shard_map/ppermute | solution.py:22
  119.0 3.0 %collective-permute-start.16 = (f32[4,4,3,262]{3,2,1,0:T(4,128)S(1)}, f32[4,4,3,262]{3,2,1,0:T(4,128)S(1)}, u32[]{:S(2)}, u32[]{:S(2)}) collective-permute-start(f32[4,4,3,262]{3,2,1,0:T(4,128)S(1)} %get-tuple-element.165), channel_id=1, source_target_pairs={{0,1},{1,2},{2,3},{3,0},{4,5},{5,6},{6,7},{7,4},{8,9},{9,10},{10,1... | collective-permute-start | bytes 150920 | tf_op jit(solution)/shard_map/ppermute | solution.py:19
  119.6 4.4 %collective-permute-start.17 = (f32[4,4,3,262]{3,2,1,0:T(4,128)}, f32[4,4,3,262]{3,2,1,0:T(4,128)}, u32[]{:S(2)}, u32[]{:S(2)}) collective-permute-start(f32[4,4,3,262]{3,2,1,0:T(4,128)} %get-tuple-element.164), channel_id=1, source_target_pairs={{1,0},{2,1},{3,2},{0,3},{5,4},{6,5},{7,6},{4,7},{9,8},{10,9},{11,1... | collective-permute-start | bytes 150920 | tf_op jit(solution)/shard_map/ppermute | solution.py:22
  127.5 9.1 %collective-permute-start.18 = (f32[4,4,32,3]{3,2,1,0:T(8,128)S(1)}, f32[4,4,32,3]{3,2,1,0:T(8,128)S(1)}, u32[]{:S(2)}, u32[]{:S(2)}) collective-permute-start(f32[4,4,32,3]{3,2,1,0:T(8,128)S(1)} %get-tuple-element.197), channel_id=1, source_target_pairs={{0,4},{4,8},{8,12},{12,16},{16,20},{20,24},{24,28},{28,0},{1,5},{5... | collective-permute-start | bytes 18440 | tf_op jit(solution)/shard_map/ppermute | solution.py:19
  131.2 12.9 %collective-permute-start.19 = (f32[4,4,32,3]{3,2,1,0:T(8,128)}, f32[4,4,32,3]{3,2,1,0:T(8,128)S(1)}, u32[]{:S(2)}, u32[]{:S(2)}) collective-permute-start(f32[4,4,32,3]{3,2,1,0:T(8,128)} %get-tuple-element.196), channel_id=1, source_target_pairs={{4,0},{8,4},{12,8},{16,12},{20,16},{24,20},{28,24},{0,28},{5,1},{9... | collective-permute-start | bytes 18440 | tf_op jit(solution)/shard_map/ppermute | solution.py:22
  (51 other events, 219.5 us)
where the time goes:
time: 149 us; the launch traced here: 148 us
  other arithmetic  41.3 us (28%)
  waiting for transfers between devices  38.2 us (26%)
  local copies, waits for them, and re-layouts  36.3 us (24%)
  starting transfers between devices  30.3 us (20%)
  between operations  1.59 us (1%)
    ppermute x10, waiting for transfers between devices, padded_2(): lax.ppermute(lax.slice_in_dim(block, 0, width, axis=dim), axis, backward)  19.5 us
    ppermute x10, starting transfers between devices, padded_2(): lax.ppermute(lax.slice_in_dim(block, 0, width, axis=dim), axis, backward)  19.4 us
    ppermute x10, waiting for transfers between devices, padded_2(): lax.ppermute(lax.slice_in_dim(block, block.shape[dim] - width, None, axis...  18.6 us
    unnamed x106, local copies, waits for them, and re-layouts  11.2 us
    ppermute x10, starting transfers between devices, padded_2(): lax.ppermute(lax.slice_in_dim(block, block.shape[dim] - width, None, axis...  10.9 us
    add_any x4, other arithmetic, face_div(): cells[1] + cells[4]  7.16 us
    scatter-add x2, local copies, waits for them, and re-layouts, fold_back(): result.at[..., col_count - rim_depth:].add(received[..., 3 * rim_depth:])  6.35 us
    mul x2, other arithmetic, face_div(): open_face * (face_speed * central - jnp.sqrt(face_speed * face_speed + 0....  4.8 us
  transfers between devices with their start and end apart: 20, of which 15 were waited for; matrix products, arithmetic and copies ran while one was open for 13% of the time, Pallas kernels for 0%

commit v1 on v0

v1 whole, which is shorter than its diff:
```python
import functools

import jax
import jax.numpy as jnp
from jax import lax
from jax.experimental import pallas as pl
from jax.experimental.pallas import tpu as pltpu
from jax.sharding import PartitionSpec as P

courant = 0.4
vert_mix = 0.1
rotation = 0.3
buoyancy = 0.3
bottom_drag = 0.2

LANES = 128
RIM = 16
MESH = pl.DeviceIdType.MESH


def exchange_kernel(state, cot, sea, lev, rows_s, rows_c, rows_n, strips, pack, depth, send, recv):
    planes, rows, cols = state.shape
    lon = lax.axis_index("lon")
    lat = lax.axis_index("lat")
    lon_n = lax.axis_size("lon")
    lat_n = lax.axis_size("lat")
    left = lax.rem(lon + lon_n - 1, lon_n)
    right = lax.rem(lon + 1, lon_n)
    has_up = lat > 0
    has_down = lat < lat_n - 1

    barrier = pltpu.get_barrier_semaphore()

    def greet(to_lon, to_lat):
        pl.semaphore_signal(barrier, inc=1, device_id=(to_lon, to_lat), device_id_type=MESH)

    greet(left, lat)
    greet(right, lat)

    @pl.when(has_up)
    def _():
        for to_lon in (left, lon, right):
            greet(to_lon, lat - 1)

    @pl.when(has_down)
    def _():
        for to_lon in (left, lon, right):
            greet(to_lon, lat + 1)

    depth[...] = (sea[...] * lev[...]).astype(jnp.float32)
    lane = lax.broadcasted_iota(jnp.int32, (rows, LANES), 1)
    for side in range(2):
        part = slice(0, LANES) if side == 0 else slice(cols - LANES, cols)
        for half in range(2):
            total = jnp.zeros((rows, LANES), jnp.float32)
            for slot in range(8):
                origin = 0 if side == 0 else LANES - 16
                moved = pltpu.roll(state[half * 8 + slot, :, part], (16 * slot - origin) % LANES, 1)
                total = jnp.where(lane // 16 == slot, moved, total)
            pack[side, :, half * LANES : (half + 1) * LANES] = total
        total = jnp.zeros((rows, LANES), jnp.float32)
        for slot in range(16):
            origin = 0 if side == 0 else LANES - 8
            moved = pltpu.roll(cot[slot, :, part], (8 * slot - origin) % LANES, 1)
            total = jnp.where(lane // 8 == slot, moved, total)
        pack[side, :, 2 * LANES : 3 * LANES] = total
        pack[side, :, 3 * LANES : 4 * LANES] = depth[:, part]

    sides = jnp.where(has_up, 1, 0) + jnp.where(has_down, 1, 0)
    pl.semaphore_wait(barrier, 2 + 3 * sides)

    def message(number, source, target, to_lon, to_lat):
        return pltpu.make_async_remote_copy(
            src_ref=source,
            dst_ref=target,
            send_sem=send.at[number],
            recv_sem=recv.at[number],
            device_id=(to_lon, to_lat),
            device_id_type=MESH,
        )

    end = rows + RIM
    sideways = [
        message(0, pack.at[0], strips.at[0, RIM:end], left, lat),
        message(1, pack.at[1], strips.at[1, RIM:end], right, lat),
    ]
    up = [
        message(2, state.at[:, 0:RIM], rows_s.at[1], lon, lat - 1),
        message(3, cot.at[:, 0:8], rows_c.at[1], lon, lat - 1),
        message(4, depth.at[0:8], rows_n.at[1], lon, lat - 1),
        message(5, pack.at[0, 0:RIM], strips.at[0, end : end + RIM], left, lat - 1),
        message(6, pack.at[1, 0:RIM], strips.at[1, end : end + RIM], right, lat - 1),
    ]
    down = [
        message(7, state.at[:, rows - RIM : rows], rows_s.at[0], lon, lat + 1),
        message(8, cot.at[:, rows - 8 : rows], rows_c.at[0], lon, lat + 1),
        message(9, depth.at[rows - 8 : rows], rows_n.at[0], lon, lat + 1),
        message(10, pack.at[0, rows - RIM : rows], strips.at[0, 0:RIM], left, lat + 1),
        message(11, pack.at[1, rows - RIM : rows], strips.at[1, 0:RIM], right, lat + 1),
    ]

    @pl.when(has_up)
    def _():
        for copy in up:
            copy.start()

    @pl.when(has_down)
    def _():
        for copy in down:
            copy.start()

    for copy in sideways:
        copy.start()
    for copy in sideways:
        copy.wait()

    @pl.when(has_up)
    def _():
        for copy in up:
            copy.wait_send()
        for copy in down:
            copy.wait_recv()

    @pl.when(has_down)
    def _():
        for copy in down:
            copy.wait_send()
        for copy in up:
            copy.wait_recv()


def exchange(state, cot, sea, lev):
    planes, rows, cols = state.shape
    f32 = jnp.float32
    return pl.pallas_call(
        exchange_kernel,
        out_shape=(
            jax.ShapeDtypeStruct((2, planes, RIM, cols), f32),
            jax.ShapeDtypeStruct((2, planes, 8, cols), f32),
            jax.ShapeDtypeStruct((2, 8, cols), f32),
            jax.ShapeDtypeStruct((2, rows + 2 * RIM, 4 * LANES), f32),
        ),
        in_specs=[pl.BlockSpec(memory_space=pltpu.VMEM)] * 4,
        out_specs=[pl.BlockSpec(memory_space=pl.ANY)] * 4,
        scratch_shapes=[
            pltpu.VMEM((2, rows, 4 * LANES), f32),
            pltpu.VMEM((rows, cols), f32),
            pltpu.SemaphoreType.DMA((12,)),
            pltpu.SemaphoreType.DMA((12,)),
        ],
        compiler_params=pltpu.CompilerParams(collective_id=0, has_side_effects=True),
        name="exchange",
    )(state, cot, sea, lev)


def step_kernel(
    lat_n, state, cot, sea, lev, rows_s, rows_c, rows_n, strips, final, adjoint,
    S, G, X1, X2, A1, FA, FB, KX, KY, WET, BOT, OX, OY, PR, W, LWY, COR,
):
    planes, rows, cols = state.shape
    levels = WET.shape[0]
    tall = rows + 2 * RIM
    tiles = cols // LANES + 1
    lat = lax.axis_index("lat")
    lane = lax.broadcasted_iota(jnp.int32, (tiles, 8, LANES), 2)
    flat_lane = lax.broadcasted_iota(jnp.int32, (8, LANES), 1)
    lat_vec = jnp.full((8, LANES), lat, jnp.int32)

    def east(v, d):
        rolled = pltpu.roll(v, (-d) % LANES, 2)
        if d > 0:
            other = jnp.concatenate([rolled[1:], rolled[:1]], axis=0)
            return jnp.where(lane < LANES - d, rolled, other)
        other = jnp.concatenate([rolled[-1:], rolled[:-1]], axis=0)
        return jnp.where(lane >= -d, rolled, other)

    def at(ref, p, r):
        return ref[p, :, pl.ds(r, 8), :]

    def put(ref, p, r, v):
        ref[p, :, pl.ds(r, 8), :] = v

    for t in range(tall // 8):
        r = 8 * t
        own = RIM <= r < rows + RIM
        slot = 0 if r < RIM else 1
        edge = (lat_vec > 0) if r < RIM else (lat_vec < lat_n - 1)

        def inside(v):
            return v if own else jnp.where(edge, v, 0.0)

        def third(tile, width, place):
            right = pltpu.roll(strips[0, r : r + 8, tile], (-width * place) % LANES, 1)
            if width * place == 0:
                right = strips[0, r : r + 8, tile]
            shift = (LANES - width - width * place) % LANES
            left = strips[1, r : r + 8, tile]
            if shift:
                left = pltpu.roll(left, shift, 1)
            return jnp.where(flat_lane < 64, right, left)

        near = RIM - 8 <= r < rows + RIM + 8
        if near:
            for j in range(tiles - 1):
                part = slice(j * LANES, (j + 1) * LANES)
                if own:
                    depth = (sea[r - RIM : r - RIM + 8, part] * lev[r - RIM : r - RIM + 8, part]).astype(
                        jnp.float32
                    )
                else:
                    depth = inside(rows_n[slot, :, part])
                for k in range(levels):
                    WET[k, j, r : r + 8, :] = (depth > k + 0.5).astype(jnp.float32)
                    BOT[k, j, r : r + 8, :] = jnp.where(jnp.abs(depth - (k + 1)) < 0.5, 1.0, 0.0)
            depth = inside(
                jnp.where(
                    flat_lane < 64,
                    strips[0, r : r + 8, 3 * LANES : 4 * LANES],
                    strips[1, r : r + 8, 3 * LANES : 4 * LANES],
                )
            )
            for k in range(levels):
                WET[k, tiles - 1, r : r + 8, :] = (depth > k + 0.5).astype(jnp.float32)
                BOT[k, tiles - 1, r : r + 8, :] = jnp.where(jnp.abs(depth - (k + 1)) < 0.5, 1.0, 0.0)
        else:
            for k in range(levels):
                WET[k, :, r : r + 8, :] = jnp.zeros((tiles, 8, LANES), jnp.float32)
        for p in range(planes):
            k = p % levels
            for j in range(tiles - 1):
                part = slice(j * LANES, (j + 1) * LANES)
                if own:
                    S[p, j, r : r + 8, :] = state[p, r - RIM : r - RIM + 8, part]
                    G[p, j, r : r + 8, :] = WET[k, j, r : r + 8, :] * cot[p, r - RIM : r - RIM + 8, part]
                else:
                    base = r if slot == 0 else r - rows - RIM
                    S[p, j, r : r + 8, :] = inside(rows_s[slot, p, base : base + 8, part])
                    if near:
                        G[p, j, r : r + 8, :] = WET[k, j, r : r + 8, :] * inside(rows_c[slot, p, :, part])
            half = p // 8
            S[p, tiles - 1, r : r + 8, :] = inside(
                third(slice(half * LANES, (half + 1) * LANES), 16, p % 8)
            )
            if near:
                G[p, tiles - 1, r : r + 8, :] = WET[k, tiles - 1, r : r + 8, :] * inside(
                    third(slice(2 * LANES, 3 * LANES), 8, p)
                )

    row = lax.broadcasted_iota(jnp.int32, (tall, LANES), 0) + (lat * rows - RIM)
    turn = jnp.pi * ((row.astype(jnp.float32) + 0.5) / (rows * lat_n) - 0.5)
    COR[...] = rotation * jnp.sin(turn)

    def sweep(first, count, body):
        def run(i, carry):
            body(first + 8 * i)
            return carry

        lax.fori_loop(0, count, run, 0)

    inner = rows // 8

    def open_faces(r):
        for k in range(levels):
            wet = at(WET, k, r)
            put(OX, k, r, wet * east(wet, 1) * (courant / 60.0))
            put(OY, k, r, wet * at(WET, k, r + 1) * (courant / 60.0))

    sweep(8, inner + 2, open_faces)

    def prepare(src, step):
        def body(r):
            press = None
            for k in range(levels):
                rho = at(WET, k, r) * (
                    (-0.2 * buoyancy) * at(src, k, r) + (0.8 * buoyancy) * at(src, levels + k, r)
                )
                press = rho if press is None else press + rho
                put(PR, k, r, press)
                u = at(src, 2 * levels + k, r)
                w = 0.5 * (u + east(u, 1))
                put(W, (step * 6) * levels + k, r, w)
                square = w * w + 0.0001
                root = lax.rsqrt(square)
                put(W, (step * 6 + 1) * levels + k, r, square * root)
                put(W, (step * 6 + 2) * levels + k, r, w * root)
                w = 0.5 * (at(src, 3 * levels + k, r) + at(src, 3 * levels + k, r + 1))
                put(W, (step * 6 + 3) * levels + k, r, w)
                square = w * w + 0.0001
                root = lax.rsqrt(square)
                put(W, (step * 6 + 4) * levels + k, r, square * root)
                put(W, (step * 6 + 5) * levels + k, r, w * root)

        sweep(8, inner + 2, body)

    def speeds(step, k, r, along):
        base = step * 6 + 3 * along
        return [at(W, (base + i) * levels + k, r) for i in range(3)]

    def stencil(c0, c1, c2, c3, c4, c5):
        central = 37.0 * (c2 + c3) - 8.0 * (c1 + c4) + (c0 + c5)
        damping = 10.0 * (c3 - c2) - 5.0 * (c4 - c1) + (c5 - c0)
        return central, damping

    def forward(src, dst, step, first, count):
        prepare(src, step)

        def body(r):
            turn = COR[pl.ds(r, 8), :][None]

            def level(k, carry):
                wet = at(WET, k, r)
                ox = at(OX, k, r)
                oy = at(OY, k, r)
                wx, sx, tx = speeds(step, k, r, 0)
                wy, sy, ty = speeds(step, k, r, 1)
                lo = jnp.maximum(k - 1, 0)
                hi = jnp.minimum(k + 1, levels - 1)
                mix_lo = vert_mix * at(WET, lo, r)
                mix_hi = vert_mix * at(WET, hi, r)
                for f in range(4):
                    p = f * levels + k
                    q = at(src, p, r)
                    c, d = stencil(east(q, -2), east(q, -1), q, east(q, 1), east(q, 2), east(q, 3))
                    put(KX, step * planes + p, r, c - tx * d)
                    flux = ox * (wx * c - sx * d)
                    total = q - (flux - east(flux, -1))
                    c, d = stencil(*[at(src, p, r + o) for o in (-2, -1)], q, *[at(src, p, r + o) for o in (1, 2, 3)])
                    put(KY, step * planes + p, r, c - ty * d)
                    flux = oy * (wy * c - sy * d)
                    put(FA, p, r, flux)
                    total = total - (flux - at(FA, p, r - 1))
                    total = total + mix_lo * (at(src, f * levels + lo, r) - q)
                    total = total + mix_hi * (at(src, f * levels + hi, r) - q)
                    if f == 2:
                        press = at(PR, k, r)
                        total = total + turn * at(src, 3 * levels + k, r)
                        total = total - 0.5 * (east(press, 1) - east(press, -1))
                        total = total - bottom_drag * at(BOT, k, r) * q
                    if f == 3:
                        total = total - turn * at(src, 2 * levels + k, r)
                        total = total - 0.5 * (at(PR, k, r + 1) - at(PR, k, r - 1))
                        total = total - bottom_drag * at(BOT, k, r) * q
                    put(dst, p, r, wet * total)
                return carry

            lax.fori_loop(0, levels, level, 0)

        sweep(first, count, body)

    def backward(grad, step, first_face, faces, first, count, store):
        def face_body(r):
            def level(k, carry):
                oy = at(OY, k, r)
                wy, sy, _ = speeds(step, k, r, 1)
                by_speed = None
                for f in range(4):
                    p = f * levels + k
                    h = oy * (at(grad, p, r + 1) - at(grad, p, r))
                    put(FA, p, r, wy * h)
                    put(FB, p, r, sy * h)
                    term = h * at(KY, step * planes + p, r)
                    by_speed = term if by_speed is None else by_speed + term
                put(LWY, k, r, by_speed)
                return carry

            lax.fori_loop(0, levels, level, 0)

        sweep(first_face, faces, face_body)

        def body(r):
            turn = COR[pl.ds(r, 8), :][None]

            def level(i, below):
                k = levels - 1 - i
                wet = at(WET, k, r)
                ox = at(OX, k, r)
                wx, sx, _ = speeds(step, k, r, 0)
                lo = jnp.maximum(k - 1, 0)
                hi = jnp.minimum(k + 1, levels - 1)
                mix_wet = vert_mix * wet
                wet_lo = jnp.where(k > 0, 1.0, 0.0) * vert_mix * at(WET, lo, r)
                wet_hi = jnp.where(k < levels - 1, 1.0, 0.0) * vert_mix * at(WET, hi, r)
                has_lo = jnp.where(k > 0, 1.0, 0.0) * mix_wet
                has_hi = jnp.where(k < levels - 1, 1.0, 0.0) * mix_wet
                keep = 1.0 - wet_lo - wet_hi
                gu = at(grad, 2 * levels + k, r)
                gv = at(grad, 3 * levels + k, r)
                by_press = 0.5 * (east(gu, 1) - east(gu, -1)) + 0.5 * (
                    at(grad, 3 * levels + k, r + 1) - at(grad, 3 * levels + k, r - 1)
                )
                below = below + by_press
                by_rho = buoyancy * wet * below
                drag = bottom_drag * at(BOT, k, r)
                speed_x = None
                sums = []
                for f in range(4):
                    p = f * levels + k
                    g = at(grad, p, r)
                    total = keep * g + has_lo * at(grad, f * levels + lo, r) + has_hi * at(grad, f * levels + hi, r)
                    h = ox * (east(g, 1) - g)
                    term = h * at(KX, step * planes + p, r)
                    speed_x = term if speed_x is None else speed_x + term
                    zw = wx * h
                    zs = sx * h
                    lr = zw + east(zw, -1)
                    le = zs - east(zs, -1)
                    both = lr + le
                    near = -9.0 * lr - 4.0 * le
                    total = total + (46.0 * lr + 6.0 * le) + (east(near, 1) + east(near, -1))
                    total = total + (east(both, 2) + east(both, -2))
                    z = [at(FA, p, r + o) for o in range(-3, 3)]
                    total = total + (37.0 * (z[2] + z[3]) - 8.0 * (z[1] + z[4]) + (z[0] + z[5]))
                    z = [at(FB, p, r + o) for o in range(-3, 3)]
                    total = total + (10.0 * (z[3] - z[2]) - 5.0 * (z[4] - z[1]) + (z[5] - z[0]))
                    sums.append(total)
                speed_y = at(LWY, k, r) + at(LWY, k, r - 1)
                sums[0] = sums[0] - 0.2 * by_rho
                sums[1] = sums[1] + 0.8 * by_rho
                sums[2] = sums[2] + 0.5 * (speed_x + east(speed_x, -1)) - turn * gv - drag * gu
                sums[3] = sums[3] + 0.5 * speed_y + turn * gu - drag * gv
                for f in range(4):
                    store(f * levels + k, r, sums[f], wet)
                return below

            lax.fori_loop(0, levels, level, jnp.zeros((tiles, 8, LANES), jnp.float32))

        sweep(first, count, body)

    forward(S, X1, 0, 8, inner + 2)
    forward(X1, X2, 1, RIM - 4, inner + 1)

    def store_middle(p, r, v, wet):
        put(A1, p, r, wet * v)

    def store_last(p, r, v, wet):
        row = pl.multiple_of(r - RIM, 8)
        for j in range(tiles - 1):
            adjoint[p, pl.ds(row, 8), j * LANES : (j + 1) * LANES] = v[j]

    backward(G, 1, 8, inner + 2, RIM - 4, inner + 1, store_middle)
    backward(A1, 0, RIM - 4, inner + 1, RIM, inner, store_last)
    for p in range(planes):
        for j in range(tiles - 1):
            final[p, :, j * LANES : (j + 1) * LANES] = X2[p, j, RIM : RIM + rows, :]


def steps(lat_n, state, cot, sea, lev, halos):
    planes, rows, cols = state.shape
    levels = planes // 4
    f32 = jnp.float32
    tall = rows + 2 * RIM
    tiles = cols // LANES + 1

    def scratch(count):
        return pltpu.VMEM((count, tiles, tall, LANES), f32)

    counts = [planes] * 7 + [2 * planes] * 2 + [levels] * 5 + [12 * levels, levels]
    return pl.pallas_call(
        functools.partial(step_kernel, lat_n),
        out_shape=(jax.ShapeDtypeStruct(state.shape, f32),) * 2,
        in_specs=[pl.BlockSpec(memory_space=pltpu.VMEM)] * 8,
        out_specs=(pl.BlockSpec(memory_space=pltpu.VMEM),) * 2,
        scratch_shapes=[scratch(count) for count in counts] + [pltpu.VMEM((tall, LANES), f32)],
        compiler_params=pltpu.CompilerParams(vmem_limit_bytes=56 * 1024 * 1024),
        name="steps",
    )(state, cot, sea, lev, *halos)


def shards(state, cotangent, seamask, levels):
    shape = state.shape
    flat = (shape[0] * shape[1], shape[2], shape[3])
    state = state.reshape(flat)
    cotangent = cotangent.reshape(flat)
    halos = exchange(state, cotangent, seamask, levels)
    final, adjoint = steps(lax.axis_size("lat"), state, cotangent, seamask, levels, halos)
    return (final.reshape(shape), adjoint.reshape(shape))


def solution(mesh):
    placed = (
        P(None, None, "lat", "lon"),
        P(None, None, "lat", "lon"),
        P("lat", "lon"),
        P("lat", "lon"),
    )
    return jax.shard_map(
        shards,
        mesh=mesh,
        in_specs=placed,
        out_specs=(P(None, None, "lat", "lon"), P(None, None, "lat", "lon")),
        check_vma=False,
    )
```

time: 149 us -> 43.7 us (0.29)
  Pallas kernels: 0 us -> 42.9 us
  other arithmetic: 41.3 us -> 0 us
  waiting for transfers between devices: 38.2 us -> 0 us
  local copies, waits for them, and re-layouts: 36.3 us -> 0 us
  starting transfers between devices: 30.3 us -> 0 us
    pallas_call x0 -> x2, Pallas kernels: none -> 42.9 us  [the longest x1 28.3 us: steps(): pl.pallas_call(functools.partial(step_kernel, lat_n), out_shape=(jax.Shap...]
    ppermute x20 -> x0, waiting for transfers between devices: 38.2 us -> none  [the longest x10 19.5 us: padded_2(): lax.ppermute(lax.slice_in_dim(block, 0, width, axis=dim), axis, backward)]
    ppermute x20 -> x0, starting transfers between devices: 30.3 us -> none  [the longest x10 19.4 us: padded_2(): lax.ppermute(lax.slice_in_dim(block, 0, width, axis=dim), axis, backward)]
    mul x21 -> x0, other arithmetic: 15.5 us -> none  [the longest x2 4.8 us: face_div(): open_face * (face_speed * central - jnp.sqrt(face_speed * face_speed + 0....]
    scatter-add x8 -> x0, local copies, waits for them, and re-layouts: 13.4 us -> none  [the longest x2 6.35 us: fold_back(): result.at[..., col_count - rim_depth:].add(received[..., 3 * rim_depth:])]
    unnamed x106 -> x0, local copies, waits for them, and re-layouts: 11.2 us -> none
    slice x20 -> x0, local copies, waits for them, and re-layouts: 10 us -> none  [the longest x4 2.65 us: slab_of(): lax.slice_in_dim(values, start, start + length, axis=values.ndim + along)]
    add_any x10 -> x0, other arithmetic: 9.15 us -> none  [the longest x4 7.16 us: face_div(): cells[1] + cells[4]]
  transfers between devices with their start and end apart: 20 -> 0, of which waited for: 15 -> 0; matrix products, arithmetic and copies ran while one was open for 13% -> 0% of each run, Pallas kernels for 0% -> 0%
where the time goes in v1:
time: 43.7 us; the launch traced here: 43.5 us
  Pallas kernels  42.9 us (98%)
  between operations  0.64 us (1%)
    pallas_call x1, Pallas kernels, steps(): pl.pallas_call(functools.partial(step_kernel, lat_n), out_shape=(jax.Shap...  28.3 us
    pallas_call x1, Pallas kernels, exchange(): pl.pallas_call(exchange_kernel, out_shape=(jax.ShapeDtypeStruct((2, plane...  14.6 us

profile of v1, /device:TPU:1, one launch (start us, length us, event | category | flops | bytes accessed | tf_op | source)
XLA Modules:
  0.0 43.5 jit_solution(9268891606630839021)
XLA Ops:
  0.6 14.6 %exchange.1 = (f32[2,16,16,256]{3,2,1,0:T(8,128)}, f32[2,16,8,256]{3,2,1,0:T(8,128)}, f32[2,8,256]{2,1,0:T(8,128)}, f32[2,64,512]{2,1,0:T(8,128)}) custom-call(f32[16,32,256]{2,1,0:T(8,128)} %bitcast.4, f32[16,32,256]{2,1,0:T(8,128)} %bitcast.6, s32[32,256]{1,0:T(8,128)} %sea.3, s32[32,256]{1,0:T(8,128)} %lev.3), custom_call_target="tpu_custom_call" | custom-call | tf_op jit(solution)/shard_map/exchange/pallas_call | solution.py:135
  15.2 28.3 %steps.1 = (f32[16,32,256]{2,1,0:T(8,128)}, f32[16,32,256]{2,1,0:T(8,128)}) custom-call(f32[16,32,256]{2,1,0:T(8,128)} %bitcast.5, f32[16,32,256]{2,1,0:T(8,128)} %bitcast.7, s32[32,256]{1,0:T(8,128)} %sea.3, s32[32,256]{1,0:T(8,128)} %lev.3, f32[2,16,16,256]{3,2,1,0:T(8,128)} %get-tuple-element.8.rows_s, f32[2,16,8,256]{3,2,1,0:T(8,128)} %get-tuple-element.9.rows_c, ...), custom_call_target="tpu_custom_call" | custom-call | tf_op jit(solution)/shard_map/steps/pallas_call | solution.py:458

commit v2 on v1

--- a/solution.py
+++ b/solution.py
@@ -2,6 +2,7 @@
 
 import jax
 import jax.numpy as jnp
+import numpy as np
 from jax import lax
 from jax.experimental import pallas as pl
 from jax.experimental.pallas import tpu as pltpu
@@ -154,19 +155,20 @@
 
 
 def step_kernel(
-    lat_n, state, cot, sea, lev, rows_s, rows_c, rows_n, strips, final, adjoint,
-    S, G, X1, X2, A1, FA, FB, KX, KY, WET, BOT, OX, OY, PR, W, LWY, COR,
+    lat_n, state, cot, sea, lev, rows_s, rows_c, rows_n, strips, ahead, behind, final, adjoint,
+    S, G, X1, X2, A1, FA, FB, LX, KX, KY, CD, WET, BOT, OX, OY, PR, W, LWY, LWX, COR, QB, ZB,
 ):
     planes, rows, cols = state.shape
     levels = WET.shape[0]
     tall = rows + 2 * RIM
     tiles = cols // LANES + 1
     lat = lax.axis_index("lat")
-    lane = lax.broadcasted_iota(jnp.int32, (tiles, 8, LANES), 2)
+    lanes = {n: lax.broadcasted_iota(jnp.int32, (tiles, n, LANES), 2) for n in (8, 16)}
     flat_lane = lax.broadcasted_iota(jnp.int32, (8, LANES), 1)
     lat_vec = jnp.full((8, LANES), lat, jnp.int32)
 
     def east(v, d):
+        lane = lanes[v.shape[1]]
         rolled = pltpu.roll(v, (-d) % LANES, 2)
         if d > 0:
             other = jnp.concatenate([rolled[1:], rolled[:1]], axis=0)
@@ -292,6 +294,67 @@
 
         sweep(8, inner + 2, body)
 
+    bands = (inner + 2) // 2
+    height = 16 * bands
+
+    def split(target, p, i, column, v):
+        high = v.astype(jnp.bfloat16)
+        low = (v - high.astype(jnp.float32)).astype(jnp.bfloat16)
+        width = tiles * LANES
+        for start, part in ((column, high), (column + width, low)):
+            target[p, 16 * i : 16 * i + 16, start : start + LANES] = part
+
+    def lon_stencils(src):
+        def part(p, carry):
+            for j in range(tiles):
+                for i in range(bands):
+                    split(QB, p, i, j * LANES, src[p, j, 8 + 16 * i : 24 + 16 * i, :])
+            return carry
+
+        lax.fori_loop(0, planes, part, 0)
+        left = QB[...].reshape(planes * height, 2 * tiles * LANES)
+        for t in range(tiles):
+            got = jnp.dot(
+                left, ahead[:, 2 * t * LANES : 2 * (t + 1) * LANES], preferred_element_type=jnp.float32
+            )
+            for half in range(2):
+                CD[:, 2 * t + half, 8 : 8 + height, :] = got[:, half * LANES : (half + 1) * LANES].reshape(
+                    planes, height, LANES
+                )
+
+    def lon_transposed(grad, step):
+        def part(k, carry):
+            for i in range(bands):
+                rows_i = slice(8 + 16 * i, 24 + 16 * i)
+                base = step * 6
+                ox = OX[k, :, rows_i, :]
+                wx = W[base * levels + k, :, rows_i, :]
+                sx = W[(base + 1) * levels + k, :, rows_i, :]
+                by_speed = None
+                for f in range(4):
+                    p = f * levels + k
+                    g = grad[p, :, rows_i, :]
+                    h = ox * (east(g, 1) - g)
+                    term = h * KX[step * planes + p, :, rows_i, :]
+                    by_speed = term if by_speed is None else by_speed + term
+                    zw = wx * h
+                    zs = sx * h
+                    for j in range(tiles):
+                        split(ZB, p, i, j * LANES, zw[j])
+                        split(ZB, p, i, (2 * tiles + j) * LANES, zs[j])
+                LWX[k, :, rows_i, :] = 0.5 * (by_speed + east(by_speed, -1))
+            return carry
+
+        lax.fori_loop(0, levels, part, 0)
+        left = ZB[...].reshape(planes * height, 4 * tiles * LANES)
+        for t in range(0, tiles, 2):
+            stop = min(t + 2, tiles)
+            got = jnp.dot(left, behind[:, t * LANES : stop * LANES], preferred_element_type=jnp.float32)
+            for j in range(t, stop):
+                LX[:, j, 8 : 8 + height, :] = got[:, (j - t) * LANES : (j - t + 1) * LANES].reshape(
+                    planes, height, LANES
+                )
+
     def speeds(step, k, r, along):
         base = step * 6 + 3 * along
         return [at(W, (base + i) * levels + k, r) for i in range(3)]
@@ -303,6 +366,7 @@
 
     def forward(src, dst, step, first, count):
         prepare(src, step)
+        lon_stencils(src)
 
         def body(r):
             turn = COR[pl.ds(r, 8), :][None]
@@ -320,7 +384,8 @@
                 for f in range(4):
                     p = f * levels + k
                     q = at(src, p, r)
-                    c, d = stencil(east(q, -2), east(q, -1), q, east(q, 1), east(q, 2), east(q, 3))
+                    c = CD[p, :tiles, pl.ds(r, 8), :]
+                    d = CD[p, tiles:, pl.ds(r, 8), :]
                     put(KX, step * planes + p, r, c - tx * d)
                     flux = ox * (wx * c - sx * d)
                     total = q - (flux - east(flux, -1))
@@ -366,6 +431,7 @@
             lax.fori_loop(0, levels, level, 0)
 
         sweep(first_face, faces, face_body)
+        lon_transposed(grad, step)
 
         def body(r):
             turn = COR[pl.ds(r, 8), :][None]
@@ -373,8 +439,6 @@
             def level(i, below):
                 k = levels - 1 - i
                 wet = at(WET, k, r)
-                ox = at(OX, k, r)
-                wx, sx, _ = speeds(step, k, r, 0)
                 lo = jnp.maximum(k - 1, 0)
                 hi = jnp.minimum(k + 1, levels - 1)
                 mix_wet = vert_mix * wet
@@ -391,23 +455,12 @@
                 below = below + by_press
                 by_rho = buoyancy * wet * below
                 drag = bottom_drag * at(BOT, k, r)
-                speed_x = None
                 sums = []
                 for f in range(4):
                     p = f * levels + k
                     g = at(grad, p, r)
                     total = keep * g + has_lo * at(grad, f * levels + lo, r) + has_hi * at(grad, f * levels + hi, r)
-                    h = ox * (east(g, 1) - g)
-                    term = h * at(KX, step * planes + p, r)
-                    speed_x = term if speed_x is None else speed_x + term
-                    zw = wx * h
-                    zs = sx * h
-                    lr = zw + east(zw, -1)
-                    le = zs - east(zs, -1)
-                    both = lr + le
-                    near = -9.0 * lr - 4.0 * le
-                    total = total + (46.0 * lr + 6.0 * le) + (east(near, 1) + east(near, -1))
-                    total = total + (east(both, 2) + east(both, -2))
+                    total = total + at(LX, p, r)
                     z = [at(FA, p, r + o) for o in range(-3, 3)]
                     total = total + (37.0 * (z[2] + z[3]) - 8.0 * (z[1] + z[4]) + (z[0] + z[5]))
                     z = [at(FB, p, r + o) for o in range(-3, 3)]
@@ -416,7 +469,7 @@
                 speed_y = at(LWY, k, r) + at(LWY, k, r - 1)
                 sums[0] = sums[0] - 0.2 * by_rho
                 sums[1] = sums[1] + 0.8 * by_rho
-                sums[2] = sums[2] + 0.5 * (speed_x + east(speed_x, -1)) - turn * gv - drag * gu
+                sums[2] = sums[2] + at(LWX, k, r) - turn * gv - drag * gu
                 sums[3] = sums[3] + 0.5 * speed_y + turn * gu - drag * gv
                 for f in range(4):
                     store(f * levels + k, r, sums[f], wet)
@@ -442,6 +495,19 @@
     for p in range(planes):
         for j in range(tiles - 1):
             final[p, :, j * LANES : (j + 1) * LANES] = X2[p, j, RIM : RIM + rows, :]
+
+
+def band_matrices(width):
+    central = np.zeros((width, width), np.float32)
+    damping = np.zeros((width, width), np.float32)
+    face = np.arange(width)
+    for offset, c, d in ((-2, 1, -1), (-1, -8, 5), (0, 37, -10), (1, 37, 10), (2, -8, -5), (3, 1, 1)):
+        central[(face + offset) % width, face] = c
+        damping[(face + offset) % width, face] = d
+    both = np.concatenate([central, damping], axis=1)
+    ahead = np.concatenate([both, both], axis=0)
+    behind = np.concatenate([central.T, central.T, -damping.T, -damping.T], axis=0)
+    return jnp.asarray(ahead, jnp.bfloat16), jnp.asarray(behind, jnp.bfloat16)
 
 
 def steps(lat_n, state, cot, sea, lev, halos):
@@ -454,16 +520,23 @@
     def scratch(count):
         return pltpu.VMEM((count, tiles, tall, LANES), f32)
 
-    counts = [planes] * 7 + [2 * planes] * 2 + [levels] * 5 + [12 * levels, levels]
+    width = tiles * LANES
+    height = rows + 16
+    shapes = [scratch(count) for count in [planes] * 8 + [2 * planes] * 2]
+    shapes.append(pltpu.VMEM((planes, 2 * tiles, tall, LANES), f32))
+    shapes += [scratch(count) for count in [levels] * 5 + [12 * levels, levels, levels]]
+    shapes.append(pltpu.VMEM((tall, LANES), f32))
+    shapes.append(pltpu.VMEM((planes, height, 2 * width), jnp.bfloat16))
+    shapes.append(pltpu.VMEM((planes, height, 4 * width), jnp.bfloat16))
     return pl.pallas_call(
         functools.partial(step_kernel, lat_n),
         out_shape=(jax.ShapeDtypeStruct(state.shape, f32),) * 2,
-        in_specs=[pl.BlockSpec(memory_space=pltpu.VMEM)] * 8,
+        in_specs=[pl.BlockSpec(memory_space=pltpu.VMEM)] * 10,
         out_specs=(pl.BlockSpec(memory_space=pltpu.VMEM),) * 2,
-        scratch_shapes=[scratch(count) for count in counts] + [pltpu.VMEM((tall, LANES), f32)],
+        scratch_shapes=shapes,
         compiler_params=pltpu.CompilerParams(vmem_limit_bytes=56 * 1024 * 1024),
         name="steps",
-    )(state, cot, sea, lev, *halos)
+    )(state, cot, sea, lev, *halos, *band_matrices(width))
 
 
 def shards(state, cotangent, seamask, levels):

time: 43.7 us -> 41.9 us (0.959)
  Pallas kernels: 42.9 us -> 41.1 us
    pallas_call x1, Pallas kernels: 28.3 us -> 26.5 us  [steps(): pl.pallas_call(functools.partial(step_kernel, lat_n), out_shape=(jax.Shap...]
where the time goes in v2:
time: 41.9 us; the launch traced here: 41.7 us
  Pallas kernels  41.1 us (98%)
  between operations  0.64 us (2%)
    pallas_call x1, Pallas kernels, steps(): pl.pallas_call(functools.partial(step_kernel, lat_n), out_shape=(jax.Shap...  26.5 us
    pallas_call x1, Pallas kernels, exchange(): pl.pallas_call(exchange_kernel, out_shape=(jax.ShapeDtypeStruct((2, plane...  14.6 us

profile of v2, /device:TPU:1, one launch (start us, length us, event | category | flops | bytes accessed | tf_op | source)
XLA Modules:
  0.0 41.7 jit_solution(17801081350761534697)
XLA Ops:
  0.6 14.6 %exchange.1 = (f32[2,16,16,256]{3,2,1,0:T(8,128)}, f32[2,16,8,256]{3,2,1,0:T(8,128)}, f32[2,8,256]{2,1,0:T(8,128)}, f32[2,64,512]{2,1,0:T(8,128)}) custom-call(f32[16,32,256]{2,1,0:T(8,128)} %bitcast.4, f32[16,32,256]{2,1,0:T(8,128)} %bitcast.6, s32[32,256]{1,0:T(8,128)} %sea.3, s32[32,256]{1,0:T(8,128)} %lev.3), custom_call_target="tpu_custom_call" | custom-call | tf_op jit(solution)/shard_map/exchange/pallas_call | solution.py:136
  15.2 26.5 %steps.1 = (f32[16,32,256]{2,1,0:T(8,128)}, f32[16,32,256]{2,1,0:T(8,128)}) custom-call(f32[16,32,256]{2,1,0:T(8,128)} %bitcast.5, f32[16,32,256]{2,1,0:T(8,128)} %bitcast.7, s32[32,256]{1,0:T(8,128)} %sea.3, s32[32,256]{1,0:T(8,128)} %lev.3, f32[2,16,16,256]{3,2,1,0:T(8,128)} %get-tuple-element.8.rows_s, f32[2,16,8,256]{3,2,1,0:T(8,128)} %get-tuple-element.9.rows_c, ...), custom_call_target="tpu_custom_call" | custom-call | tf_op jit(solution)/shard_map/steps/pallas_call | solution.py:531

commit v3 on v2

--- a/solution.py
+++ b/solution.py
@@ -19,7 +19,9 @@
 MESH = pl.DeviceIdType.MESH
 
 
-def exchange_kernel(state, cot, sea, lev, rows_s, rows_c, rows_n, strips, pack, depth, send, recv):
+def exchange_kernel(
+    state, cot, sea, lev, rows_s, rows_9, rows_c, rows_n, strips, pack, ninth, depth, send, recv
+):
     planes, rows, cols = state.shape
     lon = lax.axis_index("lon")
     lat = lax.axis_index("lat")
@@ -49,6 +51,60 @@
             greet(to_lon, lat + 1)
 
     depth[...] = (sea[...] * lev[...]).astype(jnp.float32)
+    ninth[0] = state[:, 8, :]
+    ninth[1] = state[:, rows - 9, :]
+    sides = jnp.where(has_up, 1, 0) + jnp.where(has_down, 1, 0)
+    pl.semaphore_wait(barrier, 2 + 3 * sides)
+
+    def message(number, source, target, to_lon, to_lat):
+        return pltpu.make_async_remote_copy(
+            src_ref=source,
+            dst_ref=target,
+            send_sem=send.at[number],
+            recv_sem=recv.at[number],
+            device_id=(to_lon, to_lat),
+            device_id_type=MESH,
+        )
+
+    end = rows + RIM
+    sideways = [
+        message(0, pack.at[0], strips.at[0, RIM:end], left, lat),
+        message(1, pack.at[1], strips.at[1, RIM:end], right, lat),
+    ]
+    up_rows = [
+        message(2, state.at[:, 0:8], rows_s.at[1], lon, lat - 1),
+        message(12, ninth.at[0], rows_9.at[1], lon, lat - 1),
+        message(3, cot.at[:, 0:8], rows_c.at[1], lon, lat - 1),
+        message(4, depth.at[0:8], rows_n.at[1], lon, lat - 1),
+    ]
+    up_strips = [
+        message(5, pack.at[0, 0:RIM], strips.at[0, end : end + RIM], left, lat - 1),
+        message(6, pack.at[1, 0:RIM], strips.at[1, end : end + RIM], right, lat - 1),
+    ]
+    down_rows = [
+        message(7, state.at[:, rows - 8 : rows], rows_s.at[0], lon, lat + 1),
+        message(13, ninth.at[1], rows_9.at[0], lon, lat + 1),
+        message(8, cot.at[:, rows - 8 : rows], rows_c.at[0], lon, lat + 1),
+        message(9, depth.at[rows - 8 : rows], rows_n.at[0], lon, lat + 1),
+    ]
+    down_strips = [
+        message(10, pack.at[0, rows - RIM : rows], strips.at[0, 0:RIM], left, lat + 1),
+        message(11, pack.at[1, rows - RIM : rows], strips.at[1, 0:RIM], right, lat + 1),
+    ]
+
+    up = up_rows + up_strips
+    down = down_rows + down_strips
+
+    @pl.when(has_up)
+    def _():
+        for copy in up_rows:
+            copy.start()
+
+    @pl.when(has_down)
+    def _():
+        for copy in down_rows:
+            copy.start()
+
     lane = lax.broadcasted_iota(jnp.int32, (rows, LANES), 1)
     for side in range(2):
         part = slice(0, LANES) if side == 0 else slice(cols - LANES, cols)
@@ -67,51 +123,19 @@
         pack[side, :, 2 * LANES : 3 * LANES] = total
         pack[side, :, 3 * LANES : 4 * LANES] = depth[:, part]
 
-    sides = jnp.where(has_up, 1, 0) + jnp.where(has_down, 1, 0)
-    pl.semaphore_wait(barrier, 2 + 3 * sides)
-
-    def message(number, source, target, to_lon, to_lat):
-        return pltpu.make_async_remote_copy(
-            src_ref=source,
-            dst_ref=target,
-            send_sem=send.at[number],
-            recv_sem=recv.at[number],
-            device_id=(to_lon, to_lat),
-            device_id_type=MESH,
-        )
-
-    end = rows + RIM
-    sideways = [
-        message(0, pack.at[0], strips.at[0, RIM:end], left, lat),
-        message(1, pack.at[1], strips.at[1, RIM:end], right, lat),
-    ]
-    up = [
-        message(2, state.at[:, 0:RIM], rows_s.at[1], lon, lat - 1),
-        message(3, cot.at[:, 0:8], rows_c.at[1], lon, lat - 1),
-        message(4, depth.at[0:8], rows_n.at[1], lon, lat - 1),
-        message(5, pack.at[0, 0:RIM], strips.at[0, end : end + RIM], left, lat - 1),
-        message(6, pack.at[1, 0:RIM], strips.at[1, end : end + RIM], right, lat - 1),
-    ]
-    down = [
-        message(7, state.at[:, rows - RIM : rows], rows_s.at[0], lon, lat + 1),
-        message(8, cot.at[:, rows - 8 : rows], rows_c.at[0], lon, lat + 1),
-        message(9, depth.at[rows - 8 : rows], rows_n.at[0], lon, lat + 1),
-        message(10, pack.at[0, rows - RIM : rows], strips.at[0, 0:RIM], left, lat + 1),
-        message(11, pack.at[1, rows - RIM : rows], strips.at[1, 0:RIM], right, lat + 1),
-    ]
-
-    @pl.when(has_up)
-    def _():
-        for copy in up:
-            copy.start()
-
-    @pl.when(has_down)
-    def _():
-        for copy in down:
-            copy.start()
-
     for copy in sideways:
         copy.start()
+
+    @pl.when(has_up)
+    def _():
+        for copy in up_strips:
+            copy.start()
+
+    @pl.when(has_down)
+    def _():
+        for copy in down_strips:
+            copy.start()
+
     for copy in sideways:
         copy.wait()
 
@@ -136,18 +160,20 @@
     return pl.pallas_call(
         exchange_kernel,
         out_shape=(
-            jax.ShapeDtypeStruct((2, planes, RIM, cols), f32),
+            jax.ShapeDtypeStruct((2, planes, 8, cols), f32),
+            jax.ShapeDtypeStruct((2, planes, cols), f32),
             jax.ShapeDtypeStruct((2, planes, 8, cols), f32),
             jax.ShapeDtypeStruct((2, 8, cols), f32),
             jax.ShapeDtypeStruct((2, rows + 2 * RIM, 4 * LANES), f32),
         ),
         in_specs=[pl.BlockSpec(memory_space=pltpu.VMEM)] * 4,
-        out_specs=[pl.BlockSpec(memory_space=pl.ANY)] * 4,
+        out_specs=[pl.BlockSpec(memory_space=pl.ANY)] * 5,
         scratch_shapes=[
             pltpu.VMEM((2, rows, 4 * LANES), f32),
+            pltpu.VMEM((2, planes, cols), f32),
             pltpu.VMEM((rows, cols), f32),
-            pltpu.SemaphoreType.DMA((12,)),
-            pltpu.SemaphoreType.DMA((12,)),
+            pltpu.SemaphoreType.DMA((14,)),
+            pltpu.SemaphoreType.DMA((14,)),
         ],
         compiler_params=pltpu.CompilerParams(collective_id=0, has_side_effects=True),
         name="exchange",
@@ -155,7 +181,7 @@
 
 
 def step_kernel(
-    lat_n, state, cot, sea, lev, rows_s, rows_c, rows_n, strips, ahead, behind, final, adjoint,
+    lat_n, state, cot, sea, lev, rows_s, rows_9, rows_c, rows_n, strips, ahead, behind, final, adjoint,
     S, G, X1, X2, A1, FA, FB, LX, KX, KY, CD, WET, BOT, OX, OY, PR, W, LWY, LWX, COR, QB, ZB,
 ):
     planes, rows, cols = state.shape
@@ -235,10 +261,12 @@
                     S[p, j, r : r + 8, :] = state[p, r - RIM : r - RIM + 8, part]
                     G[p, j, r : r + 8, :] = WET[k, j, r : r + 8, :] * cot[p, r - RIM : r - RIM + 8, part]
                 else:
-                    base = r if slot == 0 else r - rows - RIM
-                    S[p, j, r : r + 8, :] = inside(rows_s[slot, p, base : base + 8, part])
                     if near:
+                        S[p, j, r : r + 8, :] = inside(rows_s[slot, p, :, part])
                         G[p, j, r : r + 8, :] = WET[k, j, r : r + 8, :] * inside(rows_c[slot, p, :, part])
+                    else:
+                        outer = jnp.broadcast_to(rows_9[slot, p : p + 1, part], (8, LANES))
+                        S[p, j, r : r + 8, :] = inside(outer)
             half = p // 8
             S[p, tiles - 1, r : r + 8, :] = inside(
                 third(slice(half * LANES, (half + 1) * LANES), 16, p % 8)
@@ -531,7 +559,7 @@
     return pl.pallas_call(
         functools.partial(step_kernel, lat_n),
         out_shape=(jax.ShapeDtypeStruct(state.shape, f32),) * 2,
-        in_specs=[pl.BlockSpec(memory_space=pltpu.VMEM)] * 10,
+        in_specs=[pl.BlockSpec(memory_space=pltpu.VMEM)] * 11,
         out_specs=(pl.BlockSpec(memory_space=pltpu.VMEM),) * 2,
         scratch_shapes=shapes,
         compiler_params=pltpu.CompilerParams(vmem_limit_bytes=56 * 1024 * 1024),

time: 41.9 us -> 40.6 us (0.969)
  Pallas kernels: 41.1 us -> 39.8 us
    pallas_call x1, Pallas kernels: 14.6 us -> 13.4 us  [exchange(): pl.pallas_call(exchange_kernel, out_shape=(jax.ShapeDtypeStruct((2, plane...]
where the time goes in v3:
time: 40.6 us; the launch traced here: 40.5 us
  Pallas kernels  39.8 us (98%)
  between operations  0.64 us (2%)
    pallas_call x1, Pallas kernels, steps(): pl.pallas_call(functools.partial(step_kernel, lat_n), out_shape=(jax.Shap...  26.4 us
    pallas_call x1, Pallas kernels, exchange(): pl.pallas_call(exchange_kernel, out_shape=(jax.ShapeDtypeStruct((2, plane...  13.4 us

profile of v3, /device:TPU:1, one launch (start us, length us, event | category | flops | bytes accessed | tf_op | source)
XLA Modules:
  0.0 40.5 jit_solution(228573027693917128)
XLA Ops:
  0.6 13.4 %exchange.1 = (f32[2,16,8,256]{3,2,1,0:T(8,128)}, f32[2,16,256]{2,1,0:T(8,128)}, f32[2,16,8,256]{3,2,1,0:T(8,128)}, f32[2,8,256]{2,1,0:T(8,128)}, f32[2,64,512]{2,1,0:T(8,128)}) custom-call(f32[16,32,256]{2,1,0:T(8,128)} %bitcast.4, f32[16,32,256]{2,1,0:T(8,128)} %bitcast.6, s32[32,256]{1,0:T(8,128)} %sea.3, s32[32,256]{1,0:T(8,128)} %lev.3), custom_call_target="tpu_custom_call" | custom-call | tf_op jit(solution)/shard_map/exchange/pallas_call | solution.py:160
  14.0 26.4 %steps.1 = (f32[16,32,256]{2,1,0:T(8,128)}, f32[16,32,256]{2,1,0:T(8,128)}) custom-call(f32[16,32,256]{2,1,0:T(8,128)} %bitcast.5, f32[16,32,256]{2,1,0:T(8,128)} %bitcast.7, s32[32,256]{1,0:T(8,128)} %sea.3, s32[32,256]{1,0:T(8,128)} %lev.3, f32[2,16,8,256]{3,2,1,0:T(8,128)} %get-tuple-element.9.rows_s, f32[2,16,256]{2,1,0:T(8,128)} %get-tuple-element.10.rows_9, ...), custom_call_target="tpu_custom_call" | custom-call | tf_op jit(solution)/shard_map/steps/pallas_call | solution.py:559

commit v4 on v3

--- a/solution.py
+++ b/solution.py
@@ -350,10 +350,12 @@
                     planes, height, LANES
                 )
 
-    def lon_transposed(grad, step):
+    def lon_transposed(grad, step, start, bands):
+        height = 16 * bands
+
         def part(k, carry):
             for i in range(bands):
-                rows_i = slice(8 + 16 * i, 24 + 16 * i)
+                rows_i = slice(start + 16 * i, start + 16 * i + 16)
                 base = step * 6
                 ox = OX[k, :, rows_i, :]
                 wx = W[base * levels + k, :, rows_i, :]
@@ -374,12 +376,12 @@
             return carry
 
         lax.fori_loop(0, levels, part, 0)
-        left = ZB[...].reshape(planes * height, 4 * tiles * LANES)
+        left = ZB[:, :height, :].reshape(planes * height, 4 * tiles * LANES)
         for t in range(0, tiles, 2):
             stop = min(t + 2, tiles)
             got = jnp.dot(left, behind[:, t * LANES : stop * LANES], preferred_element_type=jnp.float32)
             for j in range(t, stop):
-                LX[:, j, 8 : 8 + height, :] = got[:, (j - t) * LANES : (j - t + 1) * LANES].reshape(
+                LX[:, j, start : start + height, :] = got[:, (j - t) * LANES : (j - t + 1) * LANES].reshape(
                     planes, height, LANES
                 )
 
@@ -459,7 +461,7 @@
             lax.fori_loop(0, levels, level, 0)
 
         sweep(first_face, faces, face_body)
-        lon_transposed(grad, step)
+        lon_transposed(grad, step, 8 if step else RIM, (inner + 2 if step else inner) // 2)
 
         def body(r):
             turn = COR[pl.ds(r, 8), :][None]

time: 40.6 us -> 40 us (0.985)
  Pallas kernels: 39.8 us -> 39.2 us
    pallas_call x1, Pallas kernels: 26.4 us -> 25.8 us  [steps(): pl.pallas_call(functools.partial(step_kernel, lat_n), out_shape=(jax.Shap...]
where the time goes in v4:
time: 40 us; the launch traced here: 39.8 us
  Pallas kernels  39.2 us (98%)
  between operations  0.64 us (2%)
    pallas_call x1, Pallas kernels, steps(): pl.pallas_call(functools.partial(step_kernel, lat_n), out_shape=(jax.Shap...  25.8 us
    pallas_call x1, Pallas kernels, exchange(): pl.pallas_call(exchange_kernel, out_shape=(jax.ShapeDtypeStruct((2, plane...  13.4 us

profile of v4, /device:TPU:1, one launch (start us, length us, event | category | flops | bytes accessed | tf_op | source)
XLA Modules:
  0.0 39.8 jit_solution(2759742499570423033)
XLA Ops:
  0.6 13.4 %exchange.1 = (f32[2,16,8,256]{3,2,1,0:T(8,128)}, f32[2,16,256]{2,1,0:T(8,128)}, f32[2,16,8,256]{3,2,1,0:T(8,128)}, f32[2,8,256]{2,1,0:T(8,128)}, f32[2,64,512]{2,1,0:T(8,128)}) custom-call(f32[16,32,256]{2,1,0:T(8,128)} %bitcast.4, f32[16,32,256]{2,1,0:T(8,128)} %bitcast.6, s32[32,256]{1,0:T(8,128)} %sea.3, s32[32,256]{1,0:T(8,128)} %lev.3), custom_call_target="tpu_custom_call" | custom-call | tf_op jit(solution)/shard_map/exchange/pallas_call | solution.py:160
  14.0 25.8 %steps.1 = (f32[16,32,256]{2,1,0:T(8,128)}, f32[16,32,256]{2,1,0:T(8,128)}) custom-call(f32[16,32,256]{2,1,0:T(8,128)} %bitcast.5, f32[16,32,256]{2,1,0:T(8,128)} %bitcast.7, s32[32,256]{1,0:T(8,128)} %sea.3, s32[32,256]{1,0:T(8,128)} %lev.3, f32[2,16,8,256]{3,2,1,0:T(8,128)} %get-tuple-element.9.rows_s, f32[2,16,256]{2,1,0:T(8,128)} %get-tuple-element.10.rows_9, ...), custom_call_target="tpu_custom_call" | custom-call | tf_op jit(solution)/shard_map/steps/pallas_call | solution.py:561
